TPU v7x, 32 devices: a whole 2x2x4 slice. The times are simulated.
32 devices in a mesh: dp: 8 (over y, x, core), feat: 4 (over z).
Axes of the slice: x: 2, y: 2, z: 4, core: 2. Of those that a mesh axis runs over, the one named last changes fastest.
Arguments:
- dataset: bfloat16 [65536, 4096], P('dp', 'feat'), may hold values from -0.09375 to 0.09375
- targets: float32 [65536], P('dp'), may hold values from 0 to 1
- indices: int32 [16384], P('dp'), may hold values from 0 to 8191
- particles: bfloat16 [384, 4096], P('dp', 'feat'), may hold values from -6 to 6
- spread: int32 [1], replicated, may hold values from 2048 to 8191
Outputs:
- attraction: float32 [384, 4096], P('dp', 'feat')
- repulsion: float32 [384, 4096], P('dp', 'feat')
Inputs may be any that keep to these rules, and one draw needn't show every extreme that they name: Entry r of indices names a row within block r // 2048 of the dataset's blocks of 8192 rows.
All inputs are finite; a program needn't handle non-finite values.
Results may differ from a plain program's by a relative error of at most 0.00115.
Values may be sent and summed in bfloat16 or wider, within the bound.
A program may use at most 128 MiB of HBM per device.

v0:
```python
import jax
import jax.numpy as jnp
from jax import lax
from jax.sharding import PartitionSpec as P


def contract(left, right):
    return lax.dot_general(
        left, right, (((1,), (1,)), ((), ())), preferred_element_type=jnp.float32
    )


def exact_dot(left, right):
    return jnp.dot(left, right, precision=lax.Precision.HIGHEST)


def body(dataset, targets, indices, particles, spread):
    batch_x = jnp.take(dataset, indices, axis=0)
    batch_t = jnp.take(targets, indices, axis=0)
    data_ratio = dataset.shape[0] / indices.shape[0]
    scale_h = spread[0].astype(jnp.float32)
    all_rows = lax.all_gather(particles, "dp", axis=0, tiled=True)
    count_all = all_rows.shape[0]
    partial_value = contract(batch_x, all_rows)
    own_logits = lax.psum_scatter(
        partial_value.astype(jnp.bfloat16), "feat", scatter_dimension=1, tiled=True
    ).astype(jnp.float32)
    own_residual = (batch_t[:, None] - jax.nn.sigmoid(own_logits)).astype(jnp.bfloat16)
    residual = lax.all_gather(own_residual, "feat", axis=1, tiled=True)
    gradient = lax.psum_scatter(
        lax.dot_general(
            residual, batch_x, (((0,), (0,)), ((), ())), preferred_element_type=jnp.float32
        ),
        "dp",
        scatter_dimension=0,
        tiled=True,
    )
    theta_own = particles.astype(jnp.float32)
    score = data_ratio * gradient - theta_own
    inner_part = contract(particles, all_rows)
    norm_part = jnp.sum(jnp.square(all_rows.astype(jnp.float32)), axis=1)
    inner, sq_norms = lax.psum((inner_part, norm_part), "feat")
    own_sq = lax.dynamic_slice_in_dim(
        sq_norms, lax.axis_index("dp") * particles.shape[0], particles.shape[0]
    )
    kernel = jnp.exp(-(own_sq[:, None] + sq_norms[None, :] - 2.0 * inner) / scale_h)
    scores_all = lax.all_gather(score, "dp", axis=0, tiled=True)
    attraction = exact_dot(kernel, scores_all) / count_all
    pulled = exact_dot(kernel, all_rows.astype(jnp.float32))
    repulsion = (theta_own * jnp.sum(kernel, axis=1)[:, None] - pulled) / count_all
    return (attraction, repulsion)


def solution(mesh):
    return jax.shard_map(
        body,
        mesh=mesh,
        in_specs=(P("dp", "feat"), P("dp"), P("dp"), P("dp", "feat"), P()),
        out_specs=(P("dp", "feat"), P("dp", "feat")),
        check_vma=False,
    )
```

profile of v0, /device:TPU:0, one launch (start us, length us, event | category | flops | bytes accessed | tf_op | source)
XLA Modules:
  0.0 247.8 jit_solution(12395606545533734463)
XLA Ops:
  7.2 0.0 copy-start
  7.2 0.0 reduce-scatter.7.cloned.1.call-start
  7.2 0.7 fusion.3
  7.9 0.0 copy-start.1
  7.9 11.8 %gather_fusion = f32[2048]{0:T(1024)S(1)} fusion(f32[8192]{0:T(1024)S(1)} %copy-done, s32[2048]{0:T(1024)S(1)} %fusion.3), kind=kCustom, calls=%fused_computation | custom fusion | bytes 24576 | tf_op jit(solution)/shard_map/jit(_take)/gather | solution.py:19
  19.8 11.9 %all_gather.9 = bf16[384,1024]{1,0:T(8,128)(2,1)S(1)} all-gather(bf16[48,1024]{1,0:T(8,128)(2,1)S(1)} %copy-done.1), channel_id=1, replica_groups=mesh['dp'=8,'feat'=4] {'dp'}, dimensions={0}, use_global_device_ids=true | all-gather | bytes 884736 | tf_op jit(solution)/shard_map/all_gather | solution.py:22
  31.6 18.9 %gather_fusion.1 = bf16[2048,1024]{1,0:T(8,128)(2,1)} fusion(bf16[8192,1024]{1,0:T(8,128)(2,1)} %param.5, s32[2048]{0:T(1024)S(1)} %fusion.3), kind=kCustom, calls=%fused_computation.1 | custom fusion | bytes 8396800 | tf_op jit(solution)/shard_map/jit(_take)/gather | solution.py:18
  50.5 5.3 %fusion = bf16[384,2048]{1,0:T(8,128)(2,1)} fusion(bf16[384,1024]{1,0:T(8,128)(2,1)S(1)} %all_gather.9, bf16[2048,1024]{1,0:T(8,128)(2,1)} %gather_fusion.1, pred[2048]{0:T(1024)(128)(4,1)S(1)} %get-tuple-element.3), kind=kOutput, calls=%fused_computation.4 | convolution fusion | flops 1613496320 | bytes 6555648 | tf_op jit(solution)/shard_map/dot_general | solution.py:8
  55.8 0.0 reduce-scatter.7.cloned.1.call-update
  55.8 0.0 all-gather.3.cloned.1.call-start
  55.9 35.7 %reduce-scatter.7.cloned.1.call-done = bf16[96,2048]{1,0:T(8,128)(2,1)} async-done(((bf16[384,2048]{1,0:T(8,128)(2,1)}), bf16[96,2048]{1,0:T(8,128)(2,1)}) %reduce-scatter.7.cloned.1.call-update) | async-done | bytes 393232
  91.6 1.9 subtract_convert_fusion
  93.6 0.0 all-gather.3.cloned.1.call-update
  93.6 0.0 reduce-scatter.5.cloned.1.call-start
  93.6 36.2 %all-gather.3.cloned.1.call-done = bf16[2048,384]{0,1:T(8,128)(2,1)} async-done(((bf16[2048,96]{0,1:T(8,128)(2,1)}), bf16[2048,384]{0,1:T(8,128)(2,1)}) %all-gather.3.cloned.1.call-update) | async-done | bytes 1572880 | tf_op jit(solution)/shard_map/all_gather | solution.py:29
  129.8 5.7 %fusion.1 = f32[384,1024]{1,0:T(8,128)} fusion(bf16[2048,384]{0,1:T(8,128)(2,1)} %all-gather.3.cloned.1.call-done, bf16[2048,1024]{1,0:T(8,128)(2,1)} %gather_fusion.1, pred[2048]{0:T(1024)(128)(4,1)S(1)} %get-tuple-element.3), kind=kOutput, calls=%fused_computation.5 | convolution fusion | flops 1612709888 | bytes 7342080 | tf_op jit(solution)/shard_map/dot_general | solution.py:31
  135.5 0.0 reduce-scatter.5.cloned.1.call-update
  135.6 0.0 all-reduce.2.cloned.1.call-start
  135.6 1.0 fusion.7
  136.6 0.0 all-reduce.2.cloned.1.call-update
  136.6 0.0 all-gather.5.cloned.1.call-start
  136.7 36.5 %reduce-scatter.5.cloned.1.call-done = f32[48,1024]{1,0:T(8,128)} async-done(((f32[384,1024]{1,0:T(8,128)}), f32[48,1024]{1,0:T(8,128)}) %reduce-scatter.5.cloned.1.call-update) | async-done | bytes 196624 | tf_op jit(solution)/shard_map/reduce_scatter | solution.py:30
  173.1 1.6 convert_subtract_fusion
  174.8 0.0 all-gather.5.cloned.1.call-update
  175.4 0.2 multiply_reduce_fusion
  175.7 11.8 %psum.14 = f32[384]{0:T(512)S(1)} all-reduce(f32[384]{0:T(512)S(1)} %multiply_reduce_fusion), channel_id=1, replica_groups=mesh['dp'=8,'feat'=4] {'feat'}, use_global_device_ids=true, to_apply=%region_1.2 | all-reduce | flops 384 | bytes 3072 | tf_op jit(solution)/shard_map/psum | solution.py:42
  187.4 0.1 dynamic_slice.3
  187.5 22.3 %all-reduce.2.cloned.1.call-done = f32[48,384]{1,0:T(8,128)} async-done(((f32[48,384]{1,0:T(8,128)}), f32[48,384]{1,0:T(8,128)}) %all-reduce.2.cloned.1.call-update) | async-done | bytes 73744 | tf_op jit(solution)/shard_map/psum | solution.py:42
  209.8 1.1 fusion.6
  210.9 2.2 fusion.2
  213.1 24.9 %all-gather.5.cloned.1.call-done = f32[384,1024]{1,0:T(8,128)} async-done(((f32[48,1024]{1,0:T(8,128)}), f32[384,1024]{1,0:T(8,128)}) %all-gather.5.cloned.1.call-update) | async-done | bytes 1572880 | tf_op jit(solution)/shard_map/all_gather | solution.py:47
  238.0 3.2 %convolution_multiply_fusion = f32[48,1024]{1,0:T(8,128)} fusion(f32[384,1024]{1,0:T(8,128)} %all-gather.5.cloned.1.call-done, f32[48,384]{1,0:T(8,128)} %all-reduce.2.cloned.1.call-done, f32[]{:T(128)} %bitcast, f32[384]{0:T(512)S(1)} %psum.14, f32[48]{0:T(128)S(1)} %dynamic_slice.3), kind=kOutput, calls=%fused_computation.8 | convolution fusion | flops 226633728 | bytes 1844932 | tf_op jit(solution)/shard_map/dot_general | solution.py:14
  (5 shorter events, 0.0 us)
Async XLA Ops:
  7.2 0.8 copy-start
  7.2 84.4 %reduce-scatter.7.cloned.1.call-start = ((), (), s32[]{:S(2)}) async-start(), calls=%async_computation.6 | async-start | bytes 1966080
  7.9 11.8 %copy-start.2 = (s32[2048]{0:T(1024)S(1)}, s32[2048]{0:T(1024)}, u32[]{:S(2)}) copy-start(s32[2048]{0:T(1024)} %param.7) | copy-start | bytes 24580
  7.9 11.8 %copy-start.1 = (bf16[48,1024]{1,0:T(8,128)(2,1)S(1)}, bf16[48,1024]{1,0:T(8,128)(2,1)}, u32[]{:S(2)}) copy-start(bf16[48,1024]{1,0:T(8,128)(2,1)} %param.8) | copy-start | bytes 294916
  55.8 74.0 %all-gather.3.cloned.1.call-start = ((), (), s32[]{:S(2)}) async-start(), calls=%async_computation.3 | async-start | bytes 1966080 | tf_op jit(solution)/shard_map/all_gather | solution.py:29
  93.6 79.5 %reduce-scatter.5.cloned.1.call-start = ((), (), s32[]{:S(2)}) async-start(), calls=%async_computation.4 | async-start | bytes 1769472 | tf_op jit(solution)/shard_map/reduce_scatter | solution.py:30
  135.6 74.3 %all-reduce.2.cloned.1.call-start = ((), (), s32[]{:S(2)}) async-start(), calls=%async_computation.2 | async-start | bytes 147456 | tf_op jit(solution)/shard_map/psum | solution.py:42
  136.6 101.4 %all-gather.5.cloned.1.call-start = ((), (), s32[]{:S(2)}) async-start(), calls=%async_computation.5 | async-start | bytes 1769472 | tf_op jit(solution)/shard_map/all_gather | solution.py:47
Sparse Core Ops, SparseCore 0:
  55.9 35.6 reduce-scatter.6
  93.7 36.0 all-gather.2
  135.7 37.4 reduce-scatter.4
  175.9 33.9 all-reduce.1
  212.3 25.6 all-gather.4
where the time goes:
time: 248 us
  waiting for transfers between devices  156 us (63%)
  local copies, waits for them, and re-layouts  30.8 us (12%)
  blocking collectives  23.6 us (10%)
  matrix products  17.3 us (7%)
  between operations  14.5 us (6%)
  other arithmetic  5.6 us (2%)
    reduce_scatter x1, waiting for transfers between devices, body(): lax.psum_scatter(lax.dot_general(residual, batch_x, (((0,), (0,)), ((), (...  36.5 us
    all_gather x1, waiting for transfers between devices, body(): residual = lax.all_gather(own_residual, 'feat', axis=1, tiled=True)  36.2 us
    unnamed x6, waiting for transfers between devices  35.8 us
    all_gather x1, waiting for transfers between devices, body(): scores_all = lax.all_gather(score, 'dp', axis=0, tiled=True)  24.9 us
    psum x1, waiting for transfers between devices, body(): inner, sq_norms = lax.psum((inner_part, norm_part), 'feat')  22.3 us
    gather x1, local copies, waits for them, and re-layouts, body(): batch_x = jnp.take(dataset, indices, axis=0)  18.9 us
    all_gather x1, blocking collectives, body(): all_rows = lax.all_gather(particles, 'dp', axis=0, tiled=True)  11.9 us
    gather x1, local copies, waits for them, and re-layouts, body(): batch_t = jnp.take(targets, indices, axis=0)  11.8 us
  transfers between devices with their start and end apart: 5, of which 5 were waited for; matrix products, arithmetic and copies ran while one was open for 2% of the time, Pallas kernels for 0%

commit v1 on v0

v1 whole, which is shorter than its diff:
```python
import functools

import jax
import jax.numpy as jnp
from jax import lax
from jax.experimental import pallas as pl
from jax.experimental.pallas import tpu as pltpu
from jax.sharding import PartitionSpec as P

MESH = pl.DeviceIdType.MESH
CHUNK = 128
LAG = 2
PIECES = 16
HELD = 4


def dot(left, right, contract=((1,), (0,)), precision=None):
    return lax.dot_general(
        left, right, (contract, ((), ())), precision=precision, preferred_element_type=jnp.float32
    )


def gather_orders(bits):
    return [list(range(1, bits)) + [0], list(range(bits - 1, 0, -1)) + [0]]


def scatter_orders(bits):
    return [[0] + list(range(1, bits)), [0] + list(range(bits - 1, 0, -1))]


def patterns(bits):
    found = [0]
    for bit in bits:
        found = found + [value | (1 << bit) for value in found]
    return sorted(found)


def kernel(
    n_dp, n_feat, ratio,
    data_hbm, targets_ref, row_ref, index_ref, own_ref, spread_ref,
    attraction_ref, repulsion_ref,
    data, pieces, x, weights, t_all, inbox, res, grad, inner_out, inner_in, kern, pulled, mixed, landing,
    data_sem, w_send, w_recv, rs_send, rs_recv, ag_send, ag_recv,
    in_send, in_recv, k_send, k_recv, g_send, g_recv,
):
    dp, z = lax.axis_index("dp"), lax.axis_index("feat")
    own, width = own_ref.shape
    half = width // 2
    count = own * n_dp
    side = count // 2
    rows = x.shape[0]
    chunks = rows // CHUNK
    bits = n_dp.bit_length() - 1

    slab = data.shape[0] // PIECES
    loads = [
        pltpu.make_async_copy(
            data_hbm.at[pl.ds(i * slab, slab)], pieces.at[i % HELD], data_sem.at[i]
        )
        for i in range(PIECES)
    ]
    for load in loads[:HELD]:
        load.start()

    barrier = pltpu.get_barrier_semaphore()
    for k in range(1, n_dp):
        pl.semaphore_signal(barrier, inc=1, device_id={"dp": dp ^ k}, device_id_type=MESH)
    for k in range(1, n_feat):
        pl.semaphore_signal(
            barrier, inc=1, device_id={"feat": lax.rem(z + k, n_feat)}, device_id_type=MESH
        )
    pl.semaphore_wait(barrier, n_dp + n_feat - 2)

    def block_rows(j):
        return pl.ds(pl.multiple_of(j * own, own), own)

    weights[block_rows(dp), :] = own_ref[...]
    w_copies = [[], []]
    number = 0
    for h, order in enumerate(gather_orders(bits)):
        for i, bit in enumerate(order):
            done = sum(1 << b for b in order[:i])
            group = []
            for pattern in patterns(order[:i]):
                j = (dp & (n_dp - 1 - done)) | pattern
                place = weights.at[block_rows(j), pl.ds(h * half, half)]
                group.append(pltpu.make_async_remote_copy(
                    src_ref=place, dst_ref=place, send_sem=w_send.at[number], recv_sem=w_recv.at[number],
                    device_id={"dp": dp ^ (1 << bit)}, device_id_type=MESH,
                ))
                number += 1
            w_copies[h].append(group)
    for h in range(2):
        for copy in w_copies[h][0]:
            copy.start()

    index_row = row_ref[...]
    table = targets_ref[...]
    for c in range(chunks):
        part = index_row[:, c * CHUNK:(c + 1) * CHUNK]
        column = lax.broadcasted_iota(jnp.int32, (128, CHUNK), 0)
        hot = jnp.where(column == part % 128, 1.0, 0.0)
        picked = dot(table, hot, precision=lax.Precision.HIGHEST)
        line = lax.broadcasted_iota(jnp.int32, picked.shape, 0)
        t_all[c] = jnp.sum(jnp.where(line == part // 128, picked, 0.0), axis=0, keepdims=True)
    grad[...] = jnp.zeros_like(grad)

    def widen_piece(i):
        loads[i].wait()

        def widen(g, _):
            start = pl.multiple_of(g * 32, 32)
            data[pl.ds(i * slab + start, 32), :] = pieces[i % HELD, pl.ds(start, 32), :].astype(jnp.float32)
            return 0

        lax.fori_loop(0, slab // 32, widen, 0)
        if i + HELD < PIECES:
            loads[i + HELD].start()

    for i in range(bits):
        for piece in range(i * PIECES // bits, (i + 1) * PIECES // bits):
            widen_piece(piece)
        for h in range(2):
            for copy in w_copies[h][i]:
                copy.wait_recv()
            if i + 1 < bits:
                for copy in w_copies[h][i + 1]:
                    copy.start()

    inner_out[pl.ds(0, own), :] = dot(own_ref[...], weights[...], ((1,), (1,)))
    squares = jnp.square(weights[...].astype(jnp.float32))
    inner_out[pl.ds(own, 8), :] = dot(
        jnp.ones((8, width), jnp.float32), squares, ((1,), (1,)), lax.Precision.HIGHEST
    )
    in_copies = [
        pltpu.make_async_remote_copy(
            src_ref=inner_out, dst_ref=inner_in.at[k - 1], send_sem=in_send.at[k - 1],
            recv_sem=in_recv.at[k - 1],
            device_id={"feat": lax.rem(z + k, n_feat)}, device_id_type=MESH,
        )
        for k in range(1, n_feat)
    ]
    for copy in in_copies:
        copy.start()

    def gather(c):
        def group(g, _):
            first = pl.multiple_of(c * CHUNK + g * 16, 16)
            place = lax.broadcasted_iota(jnp.int32, (8, width), 0)
            tiles = []
            for upper in range(2):
                tile = jnp.zeros((8, width), jnp.float32)
                for j in range(8):
                    row = data[pl.ds(index_ref[first + upper * 8 + j], 1), :]
                    tile = jnp.where(place == j, jnp.broadcast_to(row, tile.shape), tile)
                tiles.append(tile)
            x[pl.ds(first, 16), :] = jnp.concatenate(tiles, axis=0).astype(jnp.bfloat16)
            return 0

        lax.fori_loop(0, CHUNK // 16, group, 0)

    def x_chunk(c):
        return x[pl.ds(pl.multiple_of(c * CHUNK, CHUNK), CHUNK), :]

    last = n_feat - 1
    ways = [(z, 1), (last - z, -1)]

    def sum_copy(d, c):
        return pltpu.make_async_remote_copy(
            src_ref=inbox.at[d, c], dst_ref=inbox.at[d, c], send_sem=rs_send.at[d, c],
            recv_sem=rs_recv.at[d, c], device_id={"feat": z + ways[d][1]}, device_id_type=MESH,
        )

    def res_copy(d, c):
        return pltpu.make_async_remote_copy(
            src_ref=res.at[d, c], dst_ref=res.at[d, c], send_sem=ag_send.at[d, c],
            recv_sem=ag_recv.at[d, c], device_id={"feat": z - ways[d][1]}, device_id_type=MESH,
        )

    def slot(s):
        for d, (pos, _) in enumerate(ways):
            c = s - LAG * pos

            @pl.when((c >= 0) & (c < chunks))
            def _():
                part = dot(weights[d * side:(d + 1) * side, :], x_chunk(c), ((1,), (1,)))
                part = part.astype(jnp.bfloat16)

                @pl.when(pos == 0)
                def _():
                    inbox[d, c] = part
                    sum_copy(d, c).start()

                @pl.when((pos > 0) & (pos < last))
                def _():
                    sum_copy(d, c).wait_recv()
                    total = inbox[d, c].astype(jnp.float32) + part.astype(jnp.float32)
                    inbox[d, c] = total.astype(jnp.bfloat16)
                    sum_copy(d, c).start()

                @pl.when(pos == last)
                def _():
                    sum_copy(d, c).wait_recv()
                    total = inbox[d, c].astype(jnp.float32) + part.astype(jnp.float32)
                    res[d, c] = (t_all[c] - jax.nn.sigmoid(total)).astype(jnp.bfloat16)
                    res_copy(d, c).start()

        for d, (pos, _) in enumerate(ways):
            c = s - LAG * (2 * last - pos)

            @pl.when((c >= 0) & (c < chunks) & (pos < last))
            def _():
                res_copy(d, c).wait_recv()

                @pl.when(pos > 0)
                def _():
                    res_copy(d, c).start()

        @pl.when(s + 1 < chunks)
        def _():
            gather(s + 1)

        c = s - LAG * 2 * last

        @pl.when(c >= 0)
        def _():
            for d in range(2):
                grad[d * side:(d + 1) * side, :] += dot(res[d, c], x_chunk(c))

    def run(start, stop):
        def step(s, _):
            slot(s)
            return 0

        lax.fori_loop(start, stop, step, 0)

    gather(0)
    run(0, 2)

    for copy in in_copies:
        copy.wait_recv()
    inner = inner_out[...]
    for k in range(n_feat - 1):
        inner = inner + inner_in[k]
    norms, inner = inner[own:own + 1], inner[:own]
    line = lax.broadcasted_iota(jnp.int32, inner.shape, 0)
    column = lax.broadcasted_iota(jnp.int32, inner.shape, 1)
    own_norms = jnp.sum(jnp.where(column == line + dp * own, inner, 0.0), axis=1, keepdims=True)
    scale = spread_ref[0].astype(jnp.float32)
    own_kernel = jnp.exp(-(own_norms + norms - 2.0 * inner) / scale)
    kern[block_rows(dp), :] = own_kernel
    k_copies = [
        pltpu.make_async_remote_copy(
            src_ref=kern.at[block_rows(dp)], dst_ref=kern.at[block_rows(dp)], send_sem=k_send.at[k - 1],
            recv_sem=k_recv.at[k - 1], device_id={"dp": dp ^ k}, device_id_type=MESH,
        )
        for k in range(1, n_dp)
    ]
    for copy in k_copies:
        copy.start()
    coarse = own_kernel.astype(jnp.bfloat16)
    fine = (own_kernel - coarse.astype(jnp.float32)).astype(jnp.bfloat16)
    pulled[...] = dot(coarse, weights[...]) + dot(fine, weights[...])
    total = jnp.sum(own_kernel, axis=1, keepdims=True)
    repulsion_ref[...] = (own_ref[...].astype(jnp.float32) * total - pulled[...]) / count

    run(2, chunks + LAG * 2 * last)

    for copy in k_copies:
        copy.wait_recv()
    orders = scatter_orders(bits)
    g_copies = [[], []]
    number = 0
    for h, order in enumerate(orders):
        for i, bit in enumerate(order):
            done = sum(1 << b for b in order[:i])
            group = []
            for pattern in patterns(order[i + 1:]):
                kept = (dp & (done | (1 << bit))) | pattern
                sent = kept ^ (1 << bit)
                group.append((kept, number, pltpu.make_async_remote_copy(
                    src_ref=mixed.at[h, sent], dst_ref=landing.at[number], send_sem=g_send.at[number],
                    recv_sem=g_recv.at[number], device_id={"dp": dp ^ (1 << bit)}, device_id_type=MESH,
                )))
                number += 1
            g_copies[h].append(group)

    def mix(j):
        rows_j = kern[block_rows(j), :]
        for h in range(2):
            mixed[h, j] = ratio * dot(
                rows_j, grad[:, h * half:(h + 1) * half], precision=lax.Precision.HIGHEST
            )

    first = [kept for kept, _, _ in g_copies[0][0]]
    for place, kept in enumerate(first):
        mix(kept ^ 1)
        for h in range(2):
            g_copies[h][0][place][2].start()
    for kept in first:
        mix(kept)
    for i in range(bits):
        for h in range(2):
            for kept, place, copy in g_copies[h][i]:
                copy.wait_recv()
                mixed[h, kept] += landing[place]
            if i + 1 < bits:
                for _, _, copy in g_copies[h][i + 1]:
                    copy.start()
    for h in range(2):
        columns = slice(h * half, (h + 1) * half)
        attraction_ref[:, columns] = (mixed[h, dp] - pulled[:, columns]) / count

    for h in range(2):
        for group in w_copies[h]:
            for copy in group:
                copy.wait_send()
        for group in g_copies[h]:
            for _, _, copy in group:
                copy.wait_send()
    for copy in in_copies + k_copies:
        copy.wait_send()

    def drain(c, _):
        for d, (pos, _) in enumerate(ways):
            @pl.when(pos < last)
            def _():
                sum_copy(d, c).wait_send()

            @pl.when(pos > 0)
            def _():
                res_copy(d, c).wait_send()
        return 0

    lax.fori_loop(0, chunks, drain, 0)


def body(n_dp, n_feat, dataset, targets, indices, particles, spread):
    own, width = particles.shape
    count, rows = own * n_dp, indices.shape[0]
    chunks, side = rows // CHUNK, own * n_dp // 2
    vmem = pl.BlockSpec(memory_space=pltpu.VMEM)
    smem = pl.BlockSpec(memory_space=pltpu.SMEM)
    bf16, f32 = jnp.bfloat16, jnp.float32
    dma = pltpu.SemaphoreType.DMA
    steps = 2 * (n_dp - 1)
    return pl.pallas_call(
        functools.partial(kernel, n_dp, n_feat, dataset.shape[0] / rows),
        out_shape=(jax.ShapeDtypeStruct((own, width), f32),) * 2,
        in_specs=[pl.BlockSpec(memory_space=pl.ANY), vmem, vmem, smem, vmem, smem],
        out_specs=(vmem, vmem),
        scratch_shapes=[
            pltpu.VMEM(dataset.shape, f32),
            pltpu.VMEM((HELD, dataset.shape[0] // PIECES, width), bf16),
            pltpu.VMEM((rows, width), bf16),
            pltpu.VMEM((count, width), bf16),
            pltpu.VMEM((chunks, 1, CHUNK), f32),
            pltpu.VMEM((2, chunks, side, CHUNK), bf16),
            pltpu.VMEM((2, chunks, side, CHUNK), bf16),
            pltpu.VMEM((count, width), f32),
            pltpu.VMEM((own + 8, count), f32),
            pltpu.VMEM((n_feat - 1, own + 8, count), f32),
            pltpu.VMEM((count, count), f32),
            pltpu.VMEM((own, width), f32),
            pltpu.VMEM((2, n_dp, own, width // 2), f32),
            pltpu.VMEM((steps, own, width // 2), f32),
            dma((PIECES,)),
            dma((steps,)), dma((steps,)),
            dma((2, chunks)), dma((2, chunks)), dma((2, chunks)), dma((2, chunks)),
            dma((n_feat - 1,)), dma((n_feat - 1,)),
            dma((n_dp - 1,)), dma((n_dp - 1,)),
            dma((steps,)), dma((steps,)),
        ],
        compiler_params=pltpu.CompilerParams(
            collective_id=0, has_side_effects=True, vmem_limit_bytes=60 * 2**20
        ),
        cost_estimate=pl.CostEstimate(
            flops=4 * rows * count * width, bytes_accessed=2 * dataset.size, transcendentals=rows * count
        ),
    )(dataset, targets.reshape(-1, 128), indices.reshape(1, -1), indices, particles, spread)


def solution(mesh):
    return jax.shard_map(
        functools.partial(body, mesh.shape["dp"], mesh.shape["feat"]),
        mesh=mesh,
        in_specs=(P("dp", "feat"), P("dp"), P("dp"), P("dp", "feat"), P()),
        out_specs=(P("dp", "feat"), P("dp", "feat")),
        check_vma=False,
    )
```

time: 248 us -> 96.9 us (0.39)
  waiting for transfers between devices: 156 us -> 0 us
  Pallas kernels: 0 us -> 92.1 us
  local copies, waits for them, and re-layouts: 30.8 us -> 3.23 us
  blocking collectives: 23.6 us -> 0 us
  matrix products: 17.3 us -> 0 us
  between operations: 14.5 us -> 1.29 us
  other arithmetic: 5.6 us -> 0 us
    pallas_call x0 -> x1, Pallas kernels: none -> 92.1 us  [body(): pl.pallas_call(functools.partial(kernel, n_dp, n_feat, dataset.shape[0] /...]
    all_gather x2 -> x0, waiting for transfers between devices: 61.1 us -> none  [the longest x1 36.2 us: body(): residual = lax.all_gather(own_residual, 'feat', axis=1, tiled=True)]
    reduce_scatter x1 -> x0, waiting for transfers between devices: 36.5 us -> none  [body(): lax.psum_scatter(lax.dot_general(residual, batch_x, (((0,), (0,)), ((), (...]
    unnamed x6 -> x0, waiting for transfers between devices: 35.8 us -> none
    gather x2 -> x0, local copies, waits for them, and re-layouts: 30.7 us -> none  [the longest x1 18.9 us: body(): batch_x = jnp.take(dataset, indices, axis=0)]
    psum x1 -> x0, waiting for transfers between devices: 22.3 us -> none  [body(): inner, sq_norms = lax.psum((inner_part, norm_part), 'feat')]
    dot_general x5 -> x0, matrix products: 17.3 us -> none  [the longest x2 6.25 us: contract(): lax.dot_general(left, right, (((1,), (1,)), ((), ())), preferred_element_...]
    all_gather x1 -> x0, blocking collectives: 11.9 us -> none  [body(): all_rows = lax.all_gather(particles, 'dp', axis=0, tiled=True)]
  transfers between devices with their start and end apart: 5 -> 0, of which waited for: 5 -> 0; matrix products, arithmetic and copies ran while one was open for 2% -> 0% of each run, Pallas kernels for 0% -> 0%
where the time goes in v1:
time: 96.9 us; the launch traced here: 96.6 us
  Pallas kernels  92.1 us (95%)
  local copies, waits for them, and re-layouts  3.23 us (3%)
  between operations  1.29 us (1%)
    pallas_call x1, Pallas kernels, body(): pl.pallas_call(functools.partial(kernel, n_dp, n_feat, dataset.shape[0] /...  92.1 us
    unnamed x2, local copies, waits for them, and re-layouts  3.23 us

profile of v1, /device:TPU:0, one launch (start us, length us, event | category | flops | bytes accessed | tf_op | source)
XLA Modules:
  0.0 96.6 jit_solution(546688438274951249)
XLA Ops:
  1.3 92.1 %shard_map.68 = (f32[48,1024]{1,0:T(8,128)}, f32[48,1024]{1,0:T(8,128)}) custom-call(bf16[8192,1024]{1,0:T(8,128)(2,1)} %data_hbm.1, f32[64,128]{1,0:T(8,128)} %bitcast.2, s32[1,2048]{1,0:T(1,128)} %bitcast.3, s32[2048]{0:T(1024)} %index_ref.1, bf16[48,1024]{1,0:T(8,128)(2,1)} %own_ref.1, s32[1]{0:T(128)S(6)} %copy.9.spread_ref), custom_call_target="tpu_custom_call" | custom-call | flops 3221225472 | bytes 16777216 | tf_op jit(solution)/shard_map/pallas_call | solution.py:347
  93.4 1.6 %copy.10 = f32[48,1024]{1,0:T(8,128)} copy(f32[48,1024]{1,0:T(8,128)} %get-tuple-element.4) | data formatting | bytes 393216
  95.0 1.6 %copy.11 = f32[48,1024]{1,0:T(8,128)} copy(f32[48,1024]{1,0:T(8,128)} %get-tuple-element.5) | data formatting | bytes 393216

commit v2 on v1

--- a/solution.py
+++ b/solution.py
@@ -8,8 +8,8 @@
 from jax.sharding import PartitionSpec as P
 
 MESH = pl.DeviceIdType.MESH
-CHUNK = 128
-LAG = 2
+CHUNK = 256
+LAG = 1
 PIECES = 16
 HELD = 4
 
@@ -38,8 +38,8 @@
 def kernel(
     n_dp, n_feat, ratio,
     data_hbm, targets_ref, row_ref, index_ref, own_ref, spread_ref,
-    attraction_ref, repulsion_ref,
-    data, pieces, x, weights, t_all, inbox, res, grad, inner_out, inner_in, kern, pulled, mixed, landing,
+    gained_ref, pulled, scaled_ref,
+    data, pieces, x, weights, t_all, inbox, res, grad, inner_out, inner_in, kern, mixed, landing,
     data_sem, w_send, w_recv, rs_send, rs_recv, ag_send, ag_recv,
     in_send, in_recv, k_send, k_recv, g_send, g_recv,
 ):
@@ -127,22 +127,6 @@
                 for copy in w_copies[h][i + 1]:
                     copy.start()
 
-    inner_out[pl.ds(0, own), :] = dot(own_ref[...], weights[...], ((1,), (1,)))
-    squares = jnp.square(weights[...].astype(jnp.float32))
-    inner_out[pl.ds(own, 8), :] = dot(
-        jnp.ones((8, width), jnp.float32), squares, ((1,), (1,)), lax.Precision.HIGHEST
-    )
-    in_copies = [
-        pltpu.make_async_remote_copy(
-            src_ref=inner_out, dst_ref=inner_in.at[k - 1], send_sem=in_send.at[k - 1],
-            recv_sem=in_recv.at[k - 1],
-            device_id={"feat": lax.rem(z + k, n_feat)}, device_id_type=MESH,
-        )
-        for k in range(1, n_feat)
-    ]
-    for copy in in_copies:
-        copy.start()
-
     def gather(c):
         def group(g, _):
             first = pl.multiple_of(c * CHUNK + g * 16, 16)
@@ -235,7 +219,29 @@
         lax.fori_loop(start, stop, step, 0)
 
     gather(0)
-    run(0, 2)
+    run(0, 1)
+
+    inner_out[pl.ds(0, own), :] = dot(own_ref[...], weights[...], ((1,), (1,)))
+    norms = jnp.zeros((8, count), jnp.float32)
+    ones = jnp.ones((8, width // 4), jnp.bfloat16)
+    for k in range(4):
+        squares = jnp.square(weights[:, k * width // 4:(k + 1) * width // 4].astype(jnp.float32))
+        upper = squares.astype(jnp.bfloat16)
+        lower = (squares - upper.astype(jnp.float32)).astype(jnp.bfloat16)
+        norms = norms + dot(ones, upper, ((1,), (1,))) + dot(ones, lower, ((1,), (1,)))
+    inner_out[pl.ds(own, 8), :] = norms
+    in_copies = [
+        pltpu.make_async_remote_copy(
+            src_ref=inner_out, dst_ref=inner_in.at[k - 1], send_sem=in_send.at[k - 1],
+            recv_sem=in_recv.at[k - 1],
+            device_id={"feat": lax.rem(z + k, n_feat)}, device_id_type=MESH,
+        )
+        for k in range(1, n_feat)
+    ]
+    for copy in in_copies:
+        copy.start()
+
+    run(1, 3)
 
     for copy in in_copies:
         copy.wait_recv()
@@ -248,10 +254,11 @@
     own_norms = jnp.sum(jnp.where(column == line + dp * own, inner, 0.0), axis=1, keepdims=True)
     scale = spread_ref[0].astype(jnp.float32)
     own_kernel = jnp.exp(-(own_norms + norms - 2.0 * inner) / scale)
-    kern[block_rows(dp), :] = own_kernel
+    kern_rows = block_rows((dp % 2) * (n_dp // 2) + dp // 2)
+    kern[kern_rows, :] = own_kernel
     k_copies = [
         pltpu.make_async_remote_copy(
-            src_ref=kern.at[block_rows(dp)], dst_ref=kern.at[block_rows(dp)], send_sem=k_send.at[k - 1],
+            src_ref=kern.at[kern_rows], dst_ref=kern.at[kern_rows], send_sem=k_send.at[k - 1],
             recv_sem=k_recv.at[k - 1], device_id={"dp": dp ^ k}, device_id_type=MESH,
         )
         for k in range(1, n_dp)
@@ -262,9 +269,9 @@
     fine = (own_kernel - coarse.astype(jnp.float32)).astype(jnp.bfloat16)
     pulled[...] = dot(coarse, weights[...]) + dot(fine, weights[...])
     total = jnp.sum(own_kernel, axis=1, keepdims=True)
-    repulsion_ref[...] = (own_ref[...].astype(jnp.float32) * total - pulled[...]) / count
-
-    run(2, chunks + LAG * 2 * last)
+    scaled_ref[...] = own_ref[...].astype(jnp.float32) * total
+
+    run(3, chunks + LAG * 2 * last)
 
     for copy in k_copies:
         copy.wait_recv()
@@ -285,20 +292,36 @@
                 number += 1
             g_copies[h].append(group)
 
-    def mix(j):
-        rows_j = kern[block_rows(j), :]
-        for h in range(2):
-            mixed[h, j] = ratio * dot(
-                rows_j, grad[:, h * half:(h + 1) * half], precision=lax.Precision.HIGHEST
-            )
-
-    first = [kept for kept, _, _ in g_copies[0][0]]
-    for place, kept in enumerate(first):
-        mix(kept ^ 1)
-        for h in range(2):
-            g_copies[h][0][place][2].start()
-    for kept in first:
-        mix(kept)
+    for h in range(2):
+        for group in w_copies[h]:
+            for copy in group:
+                copy.wait_send()
+    for j in range(n_dp):
+        piece = slice(j * own, (j + 1) * own)
+        upper = grad[piece].astype(jnp.bfloat16)
+        weights[piece] = upper
+        x[piece] = (grad[piece] - upper.astype(jnp.float32)).astype(jnp.bfloat16)
+
+    def mix(parity):
+        taken = min(4, n_dp // 2)
+        for q in range(0, n_dp // 2, taken):
+            start = pl.multiple_of(parity * side + q * own, own)
+            rows_p = ratio * kern[pl.ds(start, taken * own), :]
+            coarse = rows_p.astype(jnp.bfloat16)
+            fine = (rows_p - coarse.astype(jnp.float32)).astype(jnp.bfloat16)
+            for h in range(2):
+                columns = slice(h * half, (h + 1) * half)
+                sums = dot(coarse, weights[:, columns]) + dot(fine, weights[:, columns])
+                sums = sums + dot(coarse, x[:count, columns])
+                for k in range(taken):
+                    mixed[h, 2 * (q + k) + parity] = sums[k * own:(k + 1) * own]
+                if parity is other and q + taken == n_dp // 2:
+                    for _, _, copy in g_copies[h][0]:
+                        copy.start()
+
+    other = 1 - dp % 2
+    mix(other)
+    mix(dp % 2)
     for i in range(bits):
         for h in range(2):
             for kept, place, copy in g_copies[h][i]:
@@ -309,12 +332,9 @@
                     copy.start()
     for h in range(2):
         columns = slice(h * half, (h + 1) * half)
-        attraction_ref[:, columns] = (mixed[h, dp] - pulled[:, columns]) / count
+        gained_ref[:, columns] = mixed[h, dp]
 
     for h in range(2):
-        for group in w_copies[h]:
-            for copy in group:
-                copy.wait_send()
         for group in g_copies[h]:
             for _, _, copy in group:
                 copy.wait_send()
@@ -344,11 +364,11 @@
     bf16, f32 = jnp.bfloat16, jnp.float32
     dma = pltpu.SemaphoreType.DMA
     steps = 2 * (n_dp - 1)
-    return pl.pallas_call(
+    gained, pulled, scaled = pl.pallas_call(
         functools.partial(kernel, n_dp, n_feat, dataset.shape[0] / rows),
-        out_shape=(jax.ShapeDtypeStruct((own, width), f32),) * 2,
+        out_shape=(jax.ShapeDtypeStruct((own, width), f32),) * 3,
         in_specs=[pl.BlockSpec(memory_space=pl.ANY), vmem, vmem, smem, vmem, smem],
-        out_specs=(vmem, vmem),
+        out_specs=(vmem, vmem, vmem),
         scratch_shapes=[
             pltpu.VMEM(dataset.shape, f32),
             pltpu.VMEM((HELD, dataset.shape[0] // PIECES, width), bf16),
@@ -361,7 +381,6 @@
             pltpu.VMEM((own + 8, count), f32),
             pltpu.VMEM((n_feat - 1, own + 8, count), f32),
             pltpu.VMEM((count, count), f32),
-            pltpu.VMEM((own, width), f32),
             pltpu.VMEM((2, n_dp, own, width // 2), f32),
             pltpu.VMEM((steps, own, width // 2), f32),
             dma((PIECES,)),
@@ -378,6 +397,7 @@
             flops=4 * rows * count * width, bytes_accessed=2 * dataset.size, transcendentals=rows * count
         ),
     )(dataset, targets.reshape(-1, 128), indices.reshape(1, -1), indices, particles, spread)
+    return (gained - pulled) / count, (scaled - pulled) / count
 
 
 def solution(mesh):

time: 96.9 us -> 93.3 us (0.963)
  local copies, waits for them, and re-layouts: 3.23 us -> 0 us
  Pallas kernels: 92.1 us -> 89.9 us
  other arithmetic: 0 us -> 1.9 us
    unnamed x2 -> x0, local copies, waits for them, and re-layouts: 3.23 us -> none
    pallas_call x1, Pallas kernels: 92.1 us -> 89.9 us  [body(): pl.pallas_call(functools.partial(kernel, n_dp, n_feat, dataset.shape[0] /...]
    div x0 -> x1, other arithmetic: none -> 1.9 us  [body(): return ((gained - pulled) / count, (scaled - pulled) / count)]
where the time goes in v2:
time: 93.3 us; the launch traced here: 93.1 us
  Pallas kernels  89.9 us (96%)
  other arithmetic  1.9 us (2%)
  between operations  1.29 us (1%)
    pallas_call x1, Pallas kernels, body(): pl.pallas_call(functools.partial(kernel, n_dp, n_feat, dataset.shape[0] /...  89.9 us
    div x1, other arithmetic, body(): return ((gained - pulled) / count, (scaled - pulled) / count)  1.9 us

profile of v2, /device:TPU:0, one launch (start us, length us, event | category | flops | bytes accessed | tf_op | source)
XLA Modules:
  0.0 93.1 jit_solution(10764124101728230899)
XLA Ops:
  1.3 89.9 %shard_map.68 = (f32[48,1024]{1,0:T(8,128)}, f32[48,1024]{1,0:T(8,128)}, f32[48,1024]{1,0:T(8,128)}) custom-call(bf16[8192,1024]{1,0:T(8,128)(2,1)} %data_hbm.1, f32[64,128]{1,0:T(8,128)} %bitcast.2, s32[1,2048]{1,0:T(1,128)} %bitcast.3, s32[2048]{0:T(1024)} %index_ref.1, bf16[48,1024]{1,0:T(8,128)(2,1)} %own_ref.1, s32[1]{0:T(128)S(6)} %copy.7.spread_ref), custom_call_target="tpu_custom_call" | custom-call | flops 3221225472 | bytes 16777216 | tf_op jit(solution)/shard_map/pallas_call | solution.py:367
  91.2 1.9 %subtract_multiply_fusion = (f32[48,1024]{1,0:T(8,128)}, f32[48,1024]{1,0:T(8,128)}) fusion(f32[48,1024]{1,0:T(8,128)} %get-tuple-element.7, f32[48,1024]{1,0:T(8,128)} %get-tuple-element.6, f32[48,1024]{1,0:T(8,128)} %get-tuple-element.5), kind=kLoop, calls=%fused_computation | loop fusion | flops 196608 | bytes 983040 | tf_op jit(solution)/shard_map/div | solution.py:400

commit v3 on v2

--- a/solution.py
+++ b/solution.py
@@ -39,7 +39,7 @@
     n_dp, n_feat, ratio,
     data_hbm, targets_ref, row_ref, index_ref, own_ref, spread_ref,
     gained_ref, pulled, scaled_ref,
-    data, pieces, x, weights, t_all, inbox, res, grad, inner_out, inner_in, kern, mixed, landing,
+    data, pieces, picked, x, weights, t_all, inbox, res, grad, inner_out, inner_in, kern, mixed, landing,
     data_sem, w_send, w_recv, rs_send, rs_recv, ag_send, ag_recv,
     in_send, in_recv, k_send, k_recv, g_send, g_recv,
 ):
@@ -100,9 +100,9 @@
         part = index_row[:, c * CHUNK:(c + 1) * CHUNK]
         column = lax.broadcasted_iota(jnp.int32, (128, CHUNK), 0)
         hot = jnp.where(column == part % 128, 1.0, 0.0)
-        picked = dot(table, hot, precision=lax.Precision.HIGHEST)
-        line = lax.broadcasted_iota(jnp.int32, picked.shape, 0)
-        t_all[c] = jnp.sum(jnp.where(line == part // 128, picked, 0.0), axis=0, keepdims=True)
+        chosen = dot(table, hot, precision=lax.Precision.HIGHEST)
+        line = lax.broadcasted_iota(jnp.int32, chosen.shape, 0)
+        t_all[c] = jnp.sum(jnp.where(line == part // 128, chosen, 0.0), axis=0, keepdims=True)
     grad[...] = jnp.zeros_like(grad)
 
     def widen_piece(i):
@@ -129,19 +129,17 @@
 
     def gather(c):
         def group(g, _):
-            first = pl.multiple_of(c * CHUNK + g * 16, 16)
-            place = lax.broadcasted_iota(jnp.int32, (8, width), 0)
-            tiles = []
-            for upper in range(2):
-                tile = jnp.zeros((8, width), jnp.float32)
-                for j in range(8):
-                    row = data[pl.ds(index_ref[first + upper * 8 + j], 1), :]
-                    tile = jnp.where(place == j, jnp.broadcast_to(row, tile.shape), tile)
-                tiles.append(tile)
-            x[pl.ds(first, 16), :] = jnp.concatenate(tiles, axis=0).astype(jnp.bfloat16)
+            start = pl.multiple_of(g * 16, 16)
+            tile = picked.at[pl.ds(start, 16)]
+            for j in range(16):
+                tile[j:j + 1, :] = data[pl.ds(index_ref[c * CHUNK + start + j], 1), :]
             return 0
 
         lax.fori_loop(0, CHUNK // 16, group, 0)
+        x[pl.ds(pl.multiple_of(c * CHUNK, CHUNK), CHUNK), :] = picked[...].astype(jnp.bfloat16)
+        for d in range(2):
+            part = dot(weights[d * side:(d + 1) * side, :], x_chunk(c), ((1,), (1,)))
+            res[d, c] = part.astype(jnp.bfloat16)
 
     def x_chunk(c):
         return x[pl.ds(pl.multiple_of(c * CHUNK, CHUNK), CHUNK), :]
@@ -167,8 +165,7 @@
 
             @pl.when((c >= 0) & (c < chunks))
             def _():
-                part = dot(weights[d * side:(d + 1) * side, :], x_chunk(c), ((1,), (1,)))
-                part = part.astype(jnp.bfloat16)
+                part = res[d, c]
 
                 @pl.when(pos == 0)
                 def _():
@@ -372,6 +369,7 @@
         scratch_shapes=[
             pltpu.VMEM(dataset.shape, f32),
             pltpu.VMEM((HELD, dataset.shape[0] // PIECES, width), bf16),
+            pltpu.VMEM((CHUNK, width), f32),
             pltpu.VMEM((rows, width), bf16),
             pltpu.VMEM((count, width), bf16),
             pltpu.VMEM((chunks, 1, CHUNK), f32),

time: 93.3 us -> 93.6 us (level)
  no operation moved by 1% of the time
where the time goes in v3:
time: 93.6 us; the launch traced here: 93.4 us
  Pallas kernels  90.2 us (96%)
  other arithmetic  1.9 us (2%)
  between operations  1.29 us (1%)
    pallas_call x1, Pallas kernels, body(): pl.pallas_call(functools.partial(kernel, n_dp, n_feat, dataset.shape[0] /...  90.2 us
    div x1, other arithmetic, body(): return ((gained - pulled) / count, (scaled - pulled) / count)  1.9 us

profile of v3, /device:TPU:0, one launch (start us, length us, event | category | flops | bytes accessed | tf_op | source)
XLA Modules:
  0.0 93.4 jit_solution(17055060460130796063)
XLA Ops:
  1.3 90.2 %shard_map.68 = (f32[48,1024]{1,0:T(8,128)}, f32[48,1024]{1,0:T(8,128)}, f32[48,1024]{1,0:T(8,128)}) custom-call(bf16[8192,1024]{1,0:T(8,128)(2,1)} %data_hbm.1, f32[64,128]{1,0:T(8,128)} %bitcast.2, s32[1,2048]{1,0:T(1,128)} %bitcast.3, s32[2048]{0:T(1024)} %index_ref.1, bf16[48,1024]{1,0:T(8,128)(2,1)} %own_ref.1, s32[1]{0:T(128)S(6)} %copy.7.spread_ref), custom_call_target="tpu_custom_call" | custom-call | flops 3221225472 | bytes 16777216 | tf_op jit(solution)/shard_map/pallas_call | solution.py:364
  91.5 1.9 %subtract_multiply_fusion = (f32[48,1024]{1,0:T(8,128)}, f32[48,1024]{1,0:T(8,128)}) fusion(f32[48,1024]{1,0:T(8,128)} %get-tuple-element.7, f32[48,1024]{1,0:T(8,128)} %get-tuple-element.6, f32[48,1024]{1,0:T(8,128)} %get-tuple-element.5), kind=kLoop, calls=%fused_computation | loop fusion | flops 196608 | bytes 983040 | tf_op jit(solution)/shard_map/div | solution.py:398
